TPU v7x, 32 devices: a whole 2x2x4 slice. The times are simulated.
32 devices in a mesh: dp: 2 (over y), ctx: 4 (over x, core), tp: 4 (over z).
Axes of the slice: x: 2, y: 2, z: 4, core: 2. Of those that a mesh axis runs over, the one named last changes fastest.
Arguments:
- queries: bfloat16 [8, 512, 4096], P(('dp', 'ctx'), None, 'tp'), may hold values from -400 to 400
- key_rows: bfloat16 [8, 512, 1024], P(('dp', 'ctx'), None, 'tp'), may hold values from -6 to 6
- value_rows: bfloat16 [8, 512, 1024], P(('dp', 'ctx'), None, 'tp'), may hold values from -6 to 6
- out_grad: bfloat16 [8, 512, 4096], P(('dp', 'ctx'), None, 'tp'), may hold values from -6 to 6
- inputs: bfloat16 [8, 512, 8192], P(('dp', 'ctx'), None, 'tp'), may hold values from -0.125 to 0.125
- doc_lengths: int32 [8, 4], P('dp'), may hold values from 1 to 160, 512 in all within a row
- doc_plan: int32 [8, 4], P('dp'), may hold values from 0 to 3, each once within a row
Outputs:
- query_grad: bfloat16 [8, 640, 4096], P(('dp', 'ctx'), None, 'tp')
- key_grad: bfloat16 [8, 640, 1024], P(('dp', 'ctx'), None, 'tp')
- value_grad: bfloat16 [8, 640, 1024], P(('dp', 'ctx'), None, 'tp')
- weight_grad: float32 [8192, 1024], P(('tp', 'dp', 'ctx'))
Inputs may be any that keep to these rules, and one draw needn't show every extreme that they name: `doc_lengths`: each row sums to 512; every document has at most 160 tokens, and one of each row has exactly 160. Each row is a permutation: document d of sequence s goes to context index doc_plan[s, d] of the same data group.
All inputs are finite; a program needn't handle non-finite values.
Results may differ from a plain program's by a relative error of at most 0.012.
Values may be sent and summed in bfloat16 or wider, within the bound.
A program may use at most 64 MiB of HBM per device.

v0:
```python
import jax
import jax.numpy as jnp
from jax import lax
from jax.sharding import PartitionSpec as P

HEADS = 32
KVH = 8
HD = 128


def head_grads(query_part, key_part, value_part, grad_part, allowed):
    score_scale = HD ** (-0.5)
    scores = (
        jnp.einsum("nrch,nsch->ncrs", query_part, key_part, preferred_element_type=jnp.float32)
        * score_scale
    )
    scores = jnp.where(allowed[:, None, :, :], scores, -jnp.inf)
    largest = jnp.max(scores, axis=3, keepdims=True)
    raised = jnp.exp(scores - largest)
    weights = raised / jnp.sum(raised, axis=3, keepdims=True)
    weights_low = weights.astype(jnp.bfloat16)
    attended = jnp.einsum(
        "ncrs,nsch->nrch", weights_low, value_part, preferred_element_type=jnp.float32
    )
    row_delta = jnp.einsum("nrch,nrch->ncr", grad_part.astype(jnp.float32), attended)
    prob_grad = jnp.einsum(
        "nrch,nsch->ncrs", grad_part, value_part, preferred_element_type=jnp.float32
    )
    dscore = (weights * (prob_grad - row_delta[..., None])).astype(jnp.bfloat16)
    query_grad = (
        jnp.einsum("ncrs,nsch->nrch", dscore, key_part, preferred_element_type=jnp.float32)
        * score_scale
    )
    key_grad = (
        jnp.einsum("ncrs,nrch->nsch", dscore, query_part, preferred_element_type=jnp.float32)
        * score_scale
    )
    value_grad = jnp.einsum(
        "ncrs,nrch->nsch", weights_low, grad_part, preferred_element_type=jnp.float32
    )
    return (query_grad, key_grad, value_grad)


def attend_blocks(query_in, key_in, value_in, grad_in, live_rows):
    blocks, capacity = live_rows.shape
    received = blocks * capacity
    kv_local = key_in.shape[1] // HD
    group_size = HEADS // KVH
    offsets = jnp.arange(capacity, dtype=jnp.int32)
    self_pair = offsets[None, None, :] == offsets[None, :, None]
    allowed = (offsets[None, None, :] <= offsets[None, :, None]) & (
        live_rows[:, :, None] | self_pair
    )
    query_stack = jnp.moveaxis(query_in.reshape(blocks, capacity, kv_local, group_size, HD), 3, 0)
    grad_stack = jnp.moveaxis(grad_in.reshape(blocks, capacity, kv_local, group_size, HD), 3, 0)
    key_part = key_in.reshape(blocks, capacity, kv_local, HD)
    value_part = value_in.reshape(blocks, capacity, kv_local, HD)

    def one_head(members):
        return head_grads(members[0], key_part, value_part, members[1], allowed)

    head_q, head_k, head_v = jax.vmap(one_head)((query_stack, grad_stack))
    query_grad = (
        jnp.moveaxis(head_q, 0, 3)
        .reshape(received, kv_local * group_size * HD)
        .astype(jnp.bfloat16)
    )
    key_grad = jnp.sum(head_k, axis=0).reshape(received, kv_local * HD).astype(jnp.bfloat16)
    value_grad = jnp.sum(head_v, axis=0).reshape(received, kv_local * HD).astype(jnp.bfloat16)
    return (query_grad, key_grad, value_grad)


def shards(queries, key_rows, value_rows, out_grad, inputs, doc_lengths, doc_plan):
    n_ctx = lax.axis_size("ctx")
    own_index = lax.axis_index("ctx")
    seq_len = queries.shape[1]
    capacity = 5 * seq_len // (4 * n_ctx)
    received = n_ctx * capacity
    starts = jnp.cumsum(doc_lengths, axis=1) - doc_lengths
    doc_ids = jnp.arange(n_ctx, dtype=jnp.int32)
    matches = (doc_plan[:, None, :] == doc_ids[None, :, None]).astype(jnp.int32)
    inverse = jnp.sum(doc_ids[None, None, :] * matches, axis=2)
    offsets = jnp.arange(capacity, dtype=jnp.int32)
    own_lengths = lax.dynamic_index_in_dim(doc_lengths, own_index, 0, keepdims=False)
    own_starts = lax.dynamic_index_in_dim(starts, own_index, 0, keepdims=False)
    outgoing = lax.dynamic_index_in_dim(inverse, own_index, 0, keepdims=False)
    send_len = jnp.take(own_lengths, outgoing)
    send_first = jnp.take(own_starts, outgoing)
    send_live = offsets[None, :] < send_len[:, None]
    send_valid = send_live.reshape(received, 1)
    send_pos = jnp.minimum(send_first[:, None] + offsets[None, :], seq_len - 1).reshape(received)

    def pack_rows(source):
        picked = jnp.take(source[0], send_pos, axis=0)
        return jnp.where(send_valid, picked, jnp.zeros((), source.dtype))

    home_q, home_k, home_v = attend_blocks(
        pack_rows(queries),
        pack_rows(key_rows),
        pack_rows(value_rows),
        pack_rows(out_grad),
        send_live,
    )
    query_grad, key_grad, value_grad = (
        lax.all_to_all(home_q, "ctx", split_axis=0, concat_axis=0, tiled=True),
        lax.all_to_all(home_k, "ctx", split_axis=0, concat_axis=0, tiled=True),
        lax.all_to_all(home_v, "ctx", split_axis=0, concat_axis=0, tiled=True),
    )
    input_rows = pack_rows(inputs)
    partial_term = jnp.einsum(
        "ra,rc->ac",
        input_rows,
        lax.all_gather(home_v, "tp", axis=1, tiled=True),
        preferred_element_type=jnp.float32,
    )
    weight_grad = lax.psum_scatter(partial_term, ("dp", "ctx"), scatter_dimension=0, tiled=True)
    return (query_grad[None], key_grad[None], value_grad[None], weight_grad)


def solution(mesh):
    placed = (
        P(("dp", "ctx"), None, "tp"),
        P(("dp", "ctx"), None, "tp"),
        P(("dp", "ctx"), None, "tp"),
        P(("dp", "ctx"), None, "tp"),
        P(("dp", "ctx"), None, "tp"),
        P("dp", None),
        P("dp", None),
    )
    return jax.shard_map(
        shards,
        mesh=mesh,
        in_specs=placed,
        out_specs=(
            P(("dp", "ctx"), None, "tp"),
            P(("dp", "ctx"), None, "tp"),
            P(("dp", "ctx"), None, "tp"),
            P(("tp", "dp", "ctx"), None),
        ),
        check_vma=False,
    )
```

profile of v0, /device:TPU:16, one launch (start us, length us, event | category | flops | bytes accessed | tf_op | source)
XLA Modules:
  0.0 189.4 jit_solution(5876831304778803960)
XLA Ops:
  7.2 1.0 reduce_window_sum.11
  8.3 0.7 sub.19
  9.0 0.8 select_reduce_fusion
  9.8 0.7 fusion.45
  10.5 0.6 gather_fusion.1
  11.1 0.6 gather_fusion.2
  12.2 3.5 %gather_fusion.5 = bf16[640,1024]{1,0:T(8,128)(2,1)} fusion(bf16[512,1024]{1,0:T(8,128)(2,1)S(1)} %bitcast.96, s32[1024]{0:T(1024)S(1)} %pad_clamp_fusion.1), kind=kCustom, calls=%fused_computation.5.clone | custom fusion | bytes 2624000 | tf_op jit(solution)/shard_map/jit(_take)/gather | solution.py:94
  15.7 5.9 %gather_fusion.4 = bf16[640,1024]{1,0:T(8,128)(2,1)} fusion(bf16[512,1024]{1,0:T(8,128)(2,1)} %bitcast.97, s32[1024]{0:T(1024)S(1)} %pad_clamp_fusion.1), kind=kCustom, calls=%fused_computation.2.clone | custom fusion | bytes 2624000 | tf_op jit(solution)/shard_map/jit(_take)/gather | solution.py:94
  21.6 3.2 %select_select_fusion = (bf16[640,1024]{1,0:T(8,128)(2,1)}, bf16[640,1024]{1,0:T(8,128)(2,1)}) fusion(bf16[640,1024]{1,0:T(8,128)(2,1)S(1)} %copy-done.6, pred[640]{0:T(1024)(128)(4,1)S(1)} %compare_and_fusion, pred[640]{0:T(1024)(128)(4,1)S(1)} %lt.72, bf16[640,1024]{1,0:T(8,128)(2,1)} %gather_fusion.4), kind=kLoop, calls=%fused_computation.41 | loop fusion | flops 2621440 | bytes 5244160 | tf_op jit(solution)/shard_map/jit(_where)/select_n | solution.py:95
  24.8 3.8 %reshape.171 = bf16[4,160,2,4,128]{4,3,2,1,0:T(4,128)(2,1)} reshape(bf16[640,1024]{1,0:T(8,128)(2,1)} %get-tuple-element.10) | data formatting | bytes 2621440 | tf_op jit(solution)/shard_map/reshape | solution.py:54
  28.6 3.2 %gather_fusion.6 = bf16[640,256]{1,0:T(8,128)(2,1)} fusion(bf16[512,256]{1,0:T(8,128)(2,1)S(1)} %bitcast.98, s32[1024]{0:T(1024)S(1)} %pad_clamp_fusion.1), kind=kCustom, calls=%fused_computation.4.clone | custom fusion | bytes 657920 | tf_op jit(solution)/shard_map/jit(_take)/gather | solution.py:94
  31.9 3.2 %gather_fusion.3 = bf16[640,256]{1,0:T(8,128)(2,1)} fusion(bf16[512,256]{1,0:T(8,128)(2,1)S(1)} %bitcast.99, s32[1024]{0:T(1024)S(1)} %pad_clamp_fusion.1), kind=kCustom, calls=%fused_computation.1.clone | custom fusion | bytes 657920 | tf_op jit(solution)/shard_map/jit(_take)/gather | solution.py:94
  35.1 2.2 %select_select_fusion.2 = (bf16[640,256]{1,0:T(8,128)(2,1)}, bf16[640,256]{1,0:T(8,128)(2,1)}) fusion(bf16[640,256]{1,0:T(8,128)(2,1)} %gather_fusion.6, pred[640]{0:T(1024)(128)(4,1)S(1)} %compare_and_fusion, pred[640]{0:T(1024)(128)(4,1)S(1)} %lt.72, bf16[640,256]{1,0:T(8,128)(2,1)} %gather_fusion.3), kind=kLoop, calls=%fused_computation.53 | loop fusion | flops 655360 | bytes 1312000 | tf_op jit(solution)/shard_map/jit(_where)/select_n | solution.py:95
  37.4 1.8 reshape.170
  39.2 3.8 %reshape.172 = bf16[4,160,2,4,128]{4,3,2,1,0:T(4,128)(2,1)} reshape(bf16[640,1024]{1,0:T(8,128)(2,1)} %get-tuple-element.9) | data formatting | bytes 2621440 | tf_op jit(solution)/shard_map/reshape | solution.py:55
  43.0 1.8 fusion.25
  44.9 1.8 fusion.52
  46.8 0.7 fusion.18
  47.5 1.7 copy-done.4
  49.2 0.7 fusion.35
  49.9 0.3 copy.74
  50.2 0.4 copy-done.9
  50.6 0.1 copy-done.12
  50.7 0.8 copy.137
  51.5 0.2 reduce-scatter.2.cloned.1.call-start
  51.9 4.1 %gather_fusion = bf16[640,2048]{1,0:T(8,128)(2,1)} fusion(bf16[512,2048]{1,0:T(8,128)(2,1)S(1)} %bitcast.95, s32[1024]{0:T(1024)S(1)} %pad_clamp_fusion), kind=kCustom, calls=%fused_computation.6 | custom fusion | bytes 5245440 | tf_op jit(solution)/shard_map/jit(_take)/gather | solution.py:94
  56.0 28.4 %all-gather.2.cloned.1.call-done = bf16[640,1024]{1,0:T(8,128)(2,1)} async-done(((bf16[640,256]{1,0:T(8,128)(2,1)}), bf16[640,1024]{1,0:T(8,128)(2,1)}) %all-gather.2.cloned.1.call-update) | async-done | bytes 1310736 | tf_op jit(solution)/shard_map/all_gather | solution.py:113
  84.4 9.0 %fusion.10 = f32[2048,1024]{1,0:T(8,128)} fusion(bf16[640,1024]{1,0:T(8,128)(2,1)} %all-gather.2.cloned.1.call-done, bf16[640,2048]{1,0:T(8,128)(2,1)} %gather_fusion, pred[640]{0:T(1024)(128)(4,1)S(1)} %compare_and_fusion, pred[640]{0:T(1024)(128)(4,1)S(1)} %lt.72), kind=kOutput, calls=%fused_computation.20 | convolution fusion | flops 2686976000 | bytes 12322048 | tf_op jit(solution)/shard_map/ra,rc->ac/dot_general | solution.py:110
  93.4 1.8 reshape.173
  95.2 4.4 %fusion.7 = f32[4,4,2,160]{3,0,2,1:T(4,128)S(1)} fusion(bf16[4,4,2,160,160]{3,4,0,2,1:T(8,128)(2,1)} %copy-done.9, bf16[4,160,2,4,128]{4,3,2,1,0:T(4,128)(2,1)} %reshape.172, bf16[4,160,2,128,1]{3,2,1,0,4:T(2,128)(2,1)} %bitcast.107), kind=kOutput, calls=%fused_computation.17 | convolution fusion | flops 211676160 | bytes 3297280 | tf_op jit(solution)/shard_map/vmap(ncrs,nsch->nrch)/dot_general | solution.py:22
  99.6 3.8 %fusion.2 = bf16[4,4,2,160,160]{3,4,0,2,1:T(8,128)(2,1)S(1)} fusion(f32[4,4,2,160]{3,0,2,1:T(4,128)S(1)} %fusion.7, f32[4,4,2,160,160]{3,4,0,2,1:T(8,128)} %copy-done.4, f32[4,4,2,160]{3,0,2,1:T(4,128)S(1)} %get-tuple-element.13, bf16[4,160,2,4,128]{4,3,2,1,0:T(4,128)(2,1)S(1)} %copy-done.11, bf16[4,160,2,128,1]{3,2,1,0,4:T(2,128)(2,1)S(1)} %bitcast.108), kind=kOutput, calls=%fused_computation.10 | convolution fusion | flops 212992000 | bytes 6594560 | tf_op jit(solution)/shard_map/vmap(nrch,nsch->ncrs)/dot_general | solution.py:26
  103.4 0.9 multiply_reduce_fusion
  104.3 0.7 copy-done.8
  105.0 0.7 copy_bitcast_fusion.2
  105.7 3.5 %all-to-all-start.1 = ((bf16[4,160,256]{2,1,0:T(8,128)(2,1)}), bf16[4,160,256]{2,1,0:T(8,128)(2,1)S(1)}, u32[]{:S(2)}, u32[]{:S(2)}) async-start(bf16[4,160,256]{2,1,0:T(8,128)(2,1)} %copy_bitcast_fusion.2), calls=%async_computation.1 | async-start | bytes 655360 | tf_op jit(solution)/shard_map/all_to_all | solution.py:106
  109.2 1.7 copy_bitcast_fusion.1
  111.0 5.0 %all-to-all-done.1 = bf16[4,160,256]{2,1,0:T(8,128)(2,1)S(1)} async-done(((bf16[4,160,256]{2,1,0:T(8,128)(2,1)}), bf16[4,160,256]{2,1,0:T(8,128)(2,1)S(1)}, u32[]{:S(2)}, u32[]{:S(2)}) %all-to-all-start.1) | async-done | bytes 327712 | tf_op jit(solution)/shard_map/all_to_all | solution.py:106
  115.9 4.1 %all-to-all-start.2 = ((bf16[4,160,256]{2,1,0:T(8,128)(2,1)}), bf16[4,160,256]{2,1,0:T(8,128)(2,1)}, u32[]{:S(2)}, u32[]{:S(2)}) async-start(bf16[4,160,256]{2,1,0:T(8,128)(2,1)} %copy_bitcast_fusion.1), calls=%async_computation.2 | async-start | bytes 655360 | tf_op jit(solution)/shard_map/all_to_all | solution.py:107
  120.1 2.9 %fusion.21 = bf16[4,160,2,4,128]{4,1,3,2,0:T(8,128)(2,1)S(1)} fusion(bf16[4,4,2,160,160]{3,4,0,2,1:T(8,128)(2,1)} %copy-done.8, bf16[4,160,2,128,1]{3,2,1,0,4:T(2,128)(2,1)S(1)} %bitcast.102), kind=kOutput, calls=%fused_computation.32 | convolution fusion | flops 211025920 | bytes 3276800 | tf_op jit(solution)/shard_map/vmap(ncrs,nsch->nrch)/dot_general | solution.py:31
  123.0 0.7 copy.71
  123.7 1.8 convert_element_type.46
  125.4 5.2 %all-to-all-done.2 = bf16[4,160,256]{2,1,0:T(8,128)(2,1)} async-done(((bf16[4,160,256]{2,1,0:T(8,128)(2,1)}), bf16[4,160,256]{2,1,0:T(8,128)(2,1)}, u32[]{:S(2)}, u32[]{:S(2)}) %all-to-all-start.2) | async-done | bytes 327712 | tf_op jit(solution)/shard_map/all_to_all | solution.py:107
  130.7 3.5 %all-to-all-start = ((bf16[4,160,1024]{2,1,0:T(8,128)(2,1)}), bf16[4,160,1024]{2,1,0:T(8,128)(2,1)S(1)}, u32[]{:S(2)}, u32[]{:S(2)}) async-start(bf16[4,160,1024]{2,1,0:T(8,128)(2,1)} %convert_element_type.46), calls=%async_computation | async-start | bytes 2621440 | tf_op jit(solution)/shard_map/all_to_all | solution.py:105
  134.2 26.8 %all-to-all-done = bf16[4,160,1024]{2,1,0:T(8,128)(2,1)S(1)} async-done(((bf16[4,160,1024]{2,1,0:T(8,128)(2,1)}), bf16[4,160,1024]{2,1,0:T(8,128)(2,1)S(1)}, u32[]{:S(2)}, u32[]{:S(2)}) %all-to-all-start) | async-done | bytes 1310752 | tf_op jit(solution)/shard_map/all_to_all | solution.py:105
  161.1 17.9 %reduce-scatter.2.cloned.1.call-done = f32[256,1024]{1,0:T(8,128)} async-done(((f32[2048,1024]{1,0:T(8,128)}), f32[256,1024]{1,0:T(8,128)}) %reduce-scatter.2.cloned.1.call-update) | async-done | bytes 1048592 | tf_op jit(solution)/shard_map/reduce_scatter | solution.py:116
  179.0 1.1 copy.141
  180.1 0.7 copy.142
  180.8 1.7 copy.143
  (46 shorter events, 0.8 us)
Async XLA Ops:
  7.2 44.7 %copy-start = (bf16[1,512,2048]{2,1,0:T(8,128)(2,1)S(1)}, bf16[1,512,2048]{2,1,0:T(8,128)(2,1)}, u32[]{:S(2)}) copy-start(bf16[1,512,2048]{2,1,0:T(8,128)(2,1)} %param.17) | copy-start | bytes 6291460
  7.2 5.0 %copy-start.1 = (bf16[1,512,1024]{2,1,0:T(8,128)(2,1)S(1)}, bf16[1,512,1024]{2,1,0:T(8,128)(2,1)}, u32[]{:S(2)}) copy-start(bf16[1,512,1024]{2,1,0:T(8,128)(2,1)} %param.16) | copy-start | bytes 3145732
  7.2 77.2 %all-gather.2.cloned.1.call-start = ((), (), s32[]{:S(2)}) async-start(), calls=%async_computation.4 | async-start | bytes 1638400 | tf_op jit(solution)/shard_map/all_gather | solution.py:113
  15.7 5.9 %copy-start.6 = (bf16[640,1024]{1,0:T(8,128)(2,1)S(1)}, bf16[640,1024]{1,0:T(8,128)(2,1)}, u32[]{:S(2)}) copy-start(bf16[640,1024]{1,0:T(8,128)(2,1)} %gather_fusion.5) | copy-start | bytes 3932164
  24.8 3.8 %copy-start.2 = (bf16[1,512,256]{2,1,0:T(8,128)(2,1)S(1)}, bf16[1,512,256]{2,1,0:T(8,128)(2,1)}, u32[]{:S(2)}) copy-start(bf16[1,512,256]{2,1,0:T(8,128)(2,1)} %param.15) | copy-start | bytes 786436
  24.8 7.1 %copy-start.3 = (bf16[1,512,256]{2,1,0:T(8,128)(2,1)S(1)}, bf16[1,512,256]{2,1,0:T(8,128)(2,1)}, u32[]{:S(2)}) copy-start(bf16[1,512,256]{2,1,0:T(8,128)(2,1)} %param.14) | copy-start | bytes 786436
  35.1 7.8 %copy-start.5 = (bf16[4,160,2,4,128]{4,3,2,1,0:T(4,128)(2,1)S(1)}, bf16[4,160,2,4,128]{4,3,2,1,0:T(4,128)(2,1)}, u32[]{:S(2)}) copy-start(bf16[4,160,2,4,128]{4,3,2,1,0:T(4,128)(2,1)} %reshape.171) | copy-start | bytes 3932164
  46.8 2.4 %copy-start.4 = (f32[4,4,2,160,160]{3,4,0,2,1:T(8,128)}, f32[4,4,2,160,160]{3,4,0,2,1:T(8,128)S(1)}, u32[]{:S(2)}) copy-start(f32[4,4,2,160,160]{3,4,0,2,1:T(8,128)S(1)} %get-tuple-element.14) | copy-start | bytes 9830404
  46.8 2.4 %copy-start.10 = (bf16[4,160,2,4,128]{4,3,2,1,0:T(4,128)(2,1)S(1)}, bf16[4,160,2,4,128]{4,3,2,1,0:T(4,128)(2,1)}, u32[]{:S(2)}) copy-start(bf16[4,160,2,4,128]{4,3,2,1,0:T(4,128)(2,1)} %reshape.172) | copy-start | bytes 3932164
  49.2 1.5 copy-start.9
  49.9 0.8 copy-start.12
  51.5 127.4 %reduce-scatter.2.cloned.1.call-start = ((), (), s32[]{:S(2)}) async-start(), calls=%async_computation.5 | async-start | bytes 9437184 | tf_op jit(solution)/shard_map/reduce_scatter | solution.py:116
  95.2 4.4 %copy-start.11 = (bf16[4,160,2,4,128]{4,3,2,1,0:T(4,128)(2,1)S(1)}, bf16[4,160,2,4,128]{4,3,2,1,0:T(4,128)(2,1)}, u32[]{:S(2)}) copy-start(bf16[4,160,2,4,128]{4,3,2,1,0:T(4,128)(2,1)} %reshape.172) | copy-start | bytes 3932164
  95.2 4.4 %copy-start.15 = (bf16[4,160,2,128]{3,2,1,0:T(2,128)(2,1)S(1)}, bf16[4,160,2,128]{3,2,1,0:T(2,128)(2,1)}, u32[]{:S(2)}) copy-start(bf16[4,160,2,128]{3,2,1,0:T(2,128)(2,1)} %reshape.173) | copy-start | bytes 983044
  103.4 1.6 copy-start.8
  105.0 15.1 %copy-start.7 = (bf16[4,160,2,128]{3,2,1,0:T(2,128)(2,1)S(1)}, bf16[4,160,2,128]{3,2,1,0:T(2,128)(2,1)}, u32[]{:S(2)}) copy-start(bf16[4,160,2,128]{3,2,1,0:T(2,128)(2,1)} %reshape.170) | copy-start | bytes 983044
  105.7 10.2 %all-to-all-start.1 = ((bf16[4,160,256]{2,1,0:T(8,128)(2,1)}), bf16[4,160,256]{2,1,0:T(8,128)(2,1)S(1)}, u32[]{:S(2)}, u32[]{:S(2)}) async-start(bf16[4,160,256]{2,1,0:T(8,128)(2,1)} %copy_bitcast_fusion.2), calls=%async_computation.1 | async-start | bytes 655360 | tf_op jit(solution)/shard_map/all_to_all | solution.py:106
  115.9 4.1 %copy-start.13 = (bf16[4,160,256]{2,1,0:T(8,128)(2,1)}, bf16[4,160,256]{2,1,0:T(8,128)(2,1)S(1)}, u32[]{:S(2)}) copy-start(bf16[4,160,256]{2,1,0:T(8,128)(2,1)S(1)} %all-to-all-done.1) | copy-start | bytes 983044
  115.9 14.7 %all-to-all-start.2 = ((bf16[4,160,256]{2,1,0:T(8,128)(2,1)}), bf16[4,160,256]{2,1,0:T(8,128)(2,1)}, u32[]{:S(2)}, u32[]{:S(2)}) async-start(bf16[4,160,256]{2,1,0:T(8,128)(2,1)} %copy_bitcast_fusion.1), calls=%async_computation.2 | async-start | bytes 655360 | tf_op jit(solution)/shard_map/all_to_all | solution.py:107
  130.7 30.4 %all-to-all-start = ((bf16[4,160,1024]{2,1,0:T(8,128)(2,1)}), bf16[4,160,1024]{2,1,0:T(8,128)(2,1)S(1)}, u32[]{:S(2)}, u32[]{:S(2)}) async-start(bf16[4,160,1024]{2,1,0:T(8,128)(2,1)} %convert_element_type.46), calls=%async_computation | async-start | bytes 2621440 | tf_op jit(solution)/shard_map/all_to_all | solution.py:105
  179.0 1.2 copy-start.14
Sparse Core Ops, SparseCore 0:
  51.7 32.6 all-gather.1
  93.6 85.3 reduce-scatter.1
where the time goes:
time: 192 us; the launch traced here: 189 us
  waiting for transfers between devices  83.4 us (43%)
  local copies, waits for them, and re-layouts  45.9 us (24%)
  matrix products  23.6 us (12%)
  between operations  14.3 us (7%)
  starting transfers between devices  11.4 us (6%)
  other arithmetic  10.9 us (6%)
    all_gather x1, waiting for transfers between devices, shards(): lax.all_gather(home_v, 'tp', axis=1, tiled=True)  28.4 us
    all_to_all x1, waiting for transfers between devices, shards(): lax.all_to_all(home_q, 'ctx', split_axis=0, concat_axis=0, tiled=True)  26.8 us
    gather x5, local copies, waits for them, and re-layouts, pack_rows(): picked = jnp.take(source[0], send_pos, axis=0)  20 us
    reduce_scatter x1, waiting for transfers between devices, shards(): lax.psum_scatter(partial_term, ('dp', 'ctx'), scatter_dimension=0, tiled=...  17.9 us
    dot_general x1, matrix products, shards(): jnp.einsum('ra,rc->ac', input_rows, lax.all_gather(home_v, 'tp', axis=1,...  9.03 us
    unnamed x36, local copies, waits for them, and re-layouts  7.36 us
    select_n x2, other arithmetic, pack_rows(): return jnp.where(send_valid, picked, jnp.zeros((), source.dtype))  5.46 us
    all_to_all x1, waiting for transfers between devices, shards(): lax.all_to_all(home_v, 'ctx', split_axis=0, concat_axis=0, tiled=True)  5.23 us
  transfers between devices with their start and end apart: 5, of which 5 were waited for; matrix products, arithmetic and copies ran while one was open for 12% of the time, Pallas kernels for 0%

commit v1 on v0

v1 whole, which is shorter than its diff:
```python
import functools

import jax
import jax.numpy as jnp
from jax import lax
from jax.experimental import pallas as pl
from jax.experimental.pallas import tpu as pltpu
from jax.sharding import PartitionSpec as P

HEADS = 32
KVH = 8
HD = 128
MESH = pl.DeviceIdType.MESH
F32 = jnp.float32
BF16 = jnp.bfloat16


def dot(a, b, ca, cb):
    return lax.dot_general(a, b, (((ca,), (cb,)), ((), ())), preferred_element_type=F32)


def attend_kernel(first_ref, len_ref, q_ref, k_ref, v_ref, g_ref, dq_ref, dk_ref, dv_ref, tok_ref, acc):
    n_blocks, cap = dq_ref.shape[0], dq_ref.shape[1]
    seq_len = q_ref.shape[0]
    kv_local = k_ref.shape[1] // HD
    group = HEADS // KVH
    scale = HD ** (-0.5)
    acc[...] = jnp.zeros_like(acc)

    def block(i, carry):
        first, length = first_ref[i], len_ref[i]
        row = lax.broadcasted_iota(jnp.int32, (cap, seq_len), 0)
        token = lax.broadcasted_iota(jnp.int32, (cap, seq_len), 1)
        pick = jnp.where((token == first + row) & (row < length), 1.0, 0.0).astype(BF16)
        row_t = lax.broadcasted_iota(jnp.int32, (seq_len, cap), 1)
        token_t = lax.broadcasted_iota(jnp.int32, (seq_len, cap), 0)
        place = jnp.where((token_t == first + row_t) & (row_t < length), 1.0, 0.0).astype(BF16)
        r = lax.broadcasted_iota(jnp.int32, (cap, cap), 0)
        c = lax.broadcasted_iota(jnp.int32, (cap, cap), 1)
        allowed = (c <= r) & ((r < length) | (c == r))
        allowed = jnp.concatenate([allowed.astype(F32)] * group, axis=0) > 0.5
        for n in range(kv_local):
            kv = slice(n * HD, (n + 1) * HD)
            wide = slice(n * group * HD, (n + 1) * group * HD)
            kb = dot(pick, k_ref[:, kv], 1, 0).astype(BF16)
            vb = dot(pick, v_ref[:, kv], 1, 0).astype(BF16)
            qw = dot(pick, q_ref[:, wide], 1, 0).astype(BF16)
            gw = dot(pick, g_ref[:, wide], 1, 0).astype(BF16)
            qb = jnp.concatenate([qw[:, h * HD:(h + 1) * HD] for h in range(group)], axis=0)
            gb = jnp.concatenate([gw[:, h * HD:(h + 1) * HD] for h in range(group)], axis=0)
            scores = jnp.where(allowed, dot(qb, kb, 1, 1) * scale, -jnp.inf)
            raised = jnp.exp(scores - jnp.max(scores, axis=1, keepdims=True))
            probs = raised / jnp.sum(raised, axis=1, keepdims=True)
            low = probs.astype(BF16)
            prob_grad = dot(gb, vb, 1, 1)
            delta = jnp.sum(low.astype(F32) * prob_grad, axis=1, keepdims=True)
            dscore = (probs * (prob_grad - delta)).astype(BF16)
            dq = (dot(dscore, kb, 1, 0) * scale).astype(BF16)
            for h in range(group):
                at = (n * group + h) * HD
                dq_ref[i, :, at:at + HD] = dq[h * cap:(h + 1) * cap]
            dk_ref[i, :, kv] = (dot(dscore, qb, 0, 0) * scale).astype(BF16)
            dv = dot(low, gb, 0, 0).astype(BF16)
            dv_ref[i, :, kv] = dv
            acc[:, kv] += dot(place, dv, 1, 0)
        return carry

    lax.fori_loop(0, n_blocks, block, 0)
    tok_ref[...] = acc[...].astype(BF16)


def exchange_kernel(
    n_dp, n_ctx, n_tp,
    dq_ref, dk_ref, dv_ref, tok_ref, x_ref,
    q_out, k_out, v_out, w_out,
    xt, vals, a_send, a_recv, keep, b_send, b_recv, c_send, c_recv,
    own_sem, ctx_ssem, ctx_rsem, z_ssem, z_rsem, a_ssem, a_rsem, b_ssem, b_rsem, c_ssem, c_rsem,
):
    dp, ctx, tp = lax.axis_index("dp"), lax.axis_index("ctx"), lax.axis_index("tp")
    n_far = n_ctx // 2
    far, near = ctx // 2, ctx % 2
    rows, width = keep.shape[3], keep.shape[4]

    def ctx_at(p):
        return (dp, lax.rem(ctx + p, n_ctx), tp)

    def tp_at(p):
        return (dp, ctx, lax.rem(tp + p, n_tp))

    def dp_at(p):
        return (lax.rem(dp + p, n_dp), ctx, tp)

    barrier = pltpu.get_barrier_semaphore()
    for p in range(1, n_ctx):
        pl.semaphore_signal(barrier, inc=1, device_id=ctx_at(p), device_id_type=MESH)
    for p in range(1, n_tp):
        pl.semaphore_signal(barrier, inc=1, device_id=tp_at(p), device_id_type=MESH)
    for p in range(1, n_dp):
        pl.semaphore_signal(barrier, inc=1, device_id=dp_at(p), device_id_type=MESH)
    pl.semaphore_wait(barrier, n_ctx + n_tp + n_dp - 3)

    def remote(src, dst, ssem, rsem, device):
        return pltpu.make_async_remote_copy(
            src_ref=src, dst_ref=dst, send_sem=ssem, recv_sem=rsem,
            device_id=device, device_id_type=MESH)

    order = [0]
    for p in range(1, n_tp // 2 + 1):
        order += [p] if 2 * p == n_tp else [p, n_tp - p]
    gathers = {}
    for p in order[1:]:
        gathers[p] = remote(tok_ref, vals.at[p], z_ssem.at[p], z_rsem.at[p], tp_at(p))
        gathers[p].start()
    moves = []
    for p in range(1, n_ctx):
        dest = lax.rem(ctx + p, n_ctx)
        for t, (src, dst) in enumerate(((dq_ref, q_out), (dk_ref, k_out), (dv_ref, v_out))):
            move = remote(src.at[dest], dst.at[ctx], ctx_ssem.at[t, p], ctx_rsem.at[t, p], ctx_at(p))
            move.start()
            moves.append(move)
    owns = []
    for t, (src, dst) in enumerate(((dq_ref, q_out), (dk_ref, k_out), (dv_ref, v_out))):
        own = pltpu.make_async_copy(src.at[ctx], dst.at[ctx], own_sem.at[t])
        own.start()
        owns.append(own)

    for b in range(n_dp * n_ctx):
        xt[b] = x_ref[:, b * rows:(b + 1) * rows].T

    near_copies, dp_copies, far_copies = {}, {}, {}
    partner = (dp, far * 2 + 1 - near, tp)

    def stage_near(u):
        p = order[u]
        if p:
            gathers[p].wait_recv()
        block = tok_ref[...] if p == 0 else vals[p]
        for d in range(n_dp):
            for f in range(n_far):
                a_send[u, d, f] = dot(xt[d * n_ctx + f * 2 + 1 - near], block, 1, 0).astype(BF16)
        near_copies[u] = remote(a_send.at[u], a_recv.at[u], a_ssem.at[u], a_rsem.at[u], partner)
        near_copies[u].start()
        for d in range(n_dp):
            for f in range(n_far):
                keep[u, d, f] = dot(xt[d * n_ctx + f * 2 + near], block, 1, 0)

    def stage_dp(u):
        near_copies[u].wait_recv()
        dp_copies[u] = []
        for p in range(1, n_dp):
            dest = lax.rem(dp + p, n_dp)
            b_send[u, p] = (keep[u, dest] + a_recv[u, dest].astype(F32)).astype(BF16)
            copy = remote(b_send.at[u, p], b_recv.at[u, p], b_ssem.at[u, p], b_rsem.at[u, p], dp_at(p))
            copy.start()
            dp_copies[u].append(copy)
        keep[u, dp] += a_recv[u, dp].astype(F32)

    def stage_far(u):
        for copy in dp_copies[u]:
            copy.wait_recv()
        far_copies[u] = []
        for p in range(1, n_far):
            dest = lax.rem(far + p, n_far)
            total = keep[u, dp, dest]
            for s in range(1, n_dp):
                total += b_recv[u, s, dest].astype(F32)
            c_send[u, p] = total.astype(BF16)
            copy = remote(
                c_send.at[u, p], c_recv.at[u, p], c_ssem.at[u, p], c_rsem.at[u, p],
                (dp, dest * 2 + near, tp))
            copy.start()
            far_copies[u].append(copy)

    def stage_last(u):
        for copy in far_copies[u]:
            copy.wait_recv()
        total = keep[u, dp, far]
        for s in range(1, n_dp):
            total += b_recv[u, s, far].astype(F32)
        for s in range(1, n_far):
            total += c_recv[u, s].astype(F32)
        source = lax.rem(tp + n_tp - order[u], n_tp)
        w_out[:, pl.ds(pl.multiple_of(source * width, width), width)] = total

    for u in range(n_tp + 3):
        for lag, stage in ((3, stage_last), (2, stage_far), (1, stage_dp), (0, stage_near)):
            if 0 <= u - lag < n_tp:
                stage(u - lag)

    for own in owns:
        own.wait()
    for move in moves:
        move.wait()
    for p in order[1:]:
        gathers[p].wait_send()
    for u in range(n_tp):
        near_copies[u].wait_send()
        for copy in dp_copies[u] + far_copies[u]:
            copy.wait_send()


def shards(queries, key_rows, value_rows, out_grad, inputs, doc_lengths, doc_plan):
    n_dp, n_ctx, n_tp = (lax.axis_size(a) for a in ("dp", "ctx", "tp"))
    own_index = lax.axis_index("ctx")
    seq_len = queries.shape[1]
    capacity = 5 * seq_len // (4 * n_ctx)
    padded = -(-capacity // 16) * 16
    q_width, kv_width, features = queries.shape[2], key_rows.shape[2], inputs.shape[2]
    n_far = n_ctx // 2
    rows = features // (n_dp * n_ctx)

    doc_ids = jnp.arange(n_ctx, dtype=jnp.int32)
    lengths = lax.dynamic_index_in_dim(doc_lengths, own_index, 0, keepdims=False)
    plan = lax.dynamic_index_in_dim(doc_plan, own_index, 0, keepdims=False)
    starts = jnp.sum(jnp.where(doc_ids[None, :] < doc_ids[:, None], lengths[None, :], 0), axis=1)
    chosen = plan[None, :] == doc_ids[:, None]
    send_len = jnp.sum(jnp.where(chosen, lengths[None, :], 0), axis=1)
    send_first = jnp.sum(jnp.where(chosen, starts[None, :], 0), axis=1)

    vmem = pl.BlockSpec(memory_space=pltpu.VMEM)
    smem = pl.BlockSpec(memory_space=pltpu.SMEM)
    anywhere = pl.BlockSpec(memory_space=pl.ANY)
    dq, dk, dv, tok = pl.pallas_call(
        attend_kernel,
        out_shape=(
            jax.ShapeDtypeStruct((n_ctx, padded, q_width), BF16),
            jax.ShapeDtypeStruct((n_ctx, padded, kv_width), BF16),
            jax.ShapeDtypeStruct((n_ctx, padded, kv_width), BF16),
            jax.ShapeDtypeStruct((seq_len, kv_width), BF16),
        ),
        in_specs=[smem, smem, vmem, vmem, vmem, vmem],
        out_specs=(vmem, vmem, vmem, vmem),
        scratch_shapes=[pltpu.VMEM((seq_len, kv_width), F32)],
        compiler_params=pltpu.CompilerParams(vmem_limit_bytes=32 << 20),
        name="attend",
    )(send_first, send_len, queries[0], key_rows[0], value_rows[0], out_grad[0])

    dma = pltpu.SemaphoreType.DMA
    q_out, k_out, v_out, w_out = pl.pallas_call(
        functools.partial(exchange_kernel, n_dp, n_ctx, n_tp),
        out_shape=(
            jax.ShapeDtypeStruct(dq.shape, BF16),
            jax.ShapeDtypeStruct(dk.shape, BF16),
            jax.ShapeDtypeStruct(dv.shape, BF16),
            jax.ShapeDtypeStruct((rows, n_tp * kv_width), F32),
        ),
        in_specs=[anywhere, anywhere, anywhere, vmem, vmem],
        out_specs=(anywhere, anywhere, anywhere, vmem),
        scratch_shapes=[
            pltpu.VMEM((n_dp * n_ctx, rows, seq_len), BF16),
            pltpu.VMEM((n_tp, seq_len, kv_width), BF16),
            pltpu.VMEM((n_tp, n_dp, n_far, rows, kv_width), BF16),
            pltpu.VMEM((n_tp, n_dp, n_far, rows, kv_width), BF16),
            pltpu.VMEM((n_tp, n_dp, n_far, rows, kv_width), F32),
            pltpu.VMEM((n_tp, n_dp, n_far, rows, kv_width), BF16),
            pltpu.VMEM((n_tp, n_dp, n_far, rows, kv_width), BF16),
            pltpu.VMEM((n_tp, n_far, rows, kv_width), BF16),
            pltpu.VMEM((n_tp, n_far, rows, kv_width), BF16),
            dma((3,)),
            dma((3, n_ctx)), dma((3, n_ctx)),
            dma((n_tp,)), dma((n_tp,)),
            dma((n_tp,)), dma((n_tp,)),
            dma((n_tp, n_dp)), dma((n_tp, n_dp)),
            dma((n_tp, n_far)), dma((n_tp, n_far)),
        ],
        compiler_params=pltpu.CompilerParams(
            collective_id=0, has_side_effects=True, vmem_limit_bytes=40 << 20),
        name="exchange",
    )(dq, dk, dv, tok, inputs[0])

    def joined(block):
        return block[:, :capacity].reshape(1, n_ctx * capacity, block.shape[2])

    return joined(q_out), joined(k_out), joined(v_out), w_out


def solution(mesh):
    rows_placed = P(("dp", "ctx"), None, "tp")
    return jax.shard_map(
        shards,
        mesh=mesh,
        in_specs=(rows_placed,) * 5 + (P("dp", None),) * 2,
        out_specs=(rows_placed, rows_placed, rows_placed, P(("tp", "dp", "ctx"), None)),
        check_vma=False,
    )
```

time: 192 us -> 72.4 us (0.38); the launches traced: 189 us -> 72.1 us
  waiting for transfers between devices: 83.4 us -> 0 us
  Pallas kernels: 0 us -> 62.6 us
  local copies, waits for them, and re-layouts: 45.9 us -> 8.54 us
  matrix products: 23.6 us -> 0 us
  between operations: 14.3 us -> 0.67 us
  starting transfers between devices: 11.4 us -> 0 us
  other arithmetic: 10.9 us -> 0.26 us
    pallas_call x0 -> x2, Pallas kernels: none -> 62.6 us  [the longest x1 51.4 us: shards(): pl.pallas_call(functools.partial(exchange_kernel, n_dp, n_ctx, n_tp), out...]
    all_to_all x3 -> x0, waiting for transfers between devices: 37 us -> none  [the longest x1 26.8 us: shards(): lax.all_to_all(home_q, 'ctx', split_axis=0, concat_axis=0, tiled=True)]
    all_gather x1 -> x0, waiting for transfers between devices: 28.4 us -> none  [shards(): lax.all_gather(home_v, 'tp', axis=1, tiled=True)]
    dot_general x7 -> x0, matrix products: 23.6 us -> none  [the longest x1 9.03 us: shards(): jnp.einsum('ra,rc->ac', input_rows, lax.all_gather(home_v, 'tp', axis=1,...]
    gather x7 -> x0, local copies, waits for them, and re-layouts: 21.2 us -> none  [the longest x5 20 us: pack_rows(): picked = jnp.take(source[0], send_pos, axis=0)]
    reduce_scatter x1 -> x0, waiting for transfers between devices: 17.9 us -> none  [shards(): lax.psum_scatter(partial_term, ('dp', 'ctx'), scatter_dimension=0, tiled=...]
    reshape x4 -> x0, local copies, waits for them, and re-layouts: 11.2 us -> none  [the longest x1 3.83 us: attend_blocks(): query_in.reshape(blocks, capacity, kv_local, group_size, HD)]
    all_to_all x3 -> x0, starting transfers between devices: 11.1 us -> none  [the longest x1 4.11 us: shards(): lax.all_to_all(home_v, 'ctx', split_axis=0, concat_axis=0, tiled=True)]
  transfers between devices with their start and end apart: 5 -> 0, of which waited for: 5 -> 0; matrix products, arithmetic and copies ran while one was open for 12% -> 0% of each run, Pallas kernels for 0% -> 0%
where the time goes in v1:
time: 72.4 us; the launch traced here: 72.1 us
  Pallas kernels  62.6 us (86%)
  local copies, waits for them, and re-layouts  8.54 us (12%)
    pallas_call x1, Pallas kernels, shards(): pl.pallas_call(functools.partial(exchange_kernel, n_dp, n_ctx, n_tp), out...  51.4 us
    pallas_call x1, Pallas kernels, shards(): pl.pallas_call(attend_kernel, out_shape=(jax.ShapeDtypeStruct((n_ctx, pad...  11.2 us
    unnamed x14, local copies, waits for them, and re-layouts  7.83 us

profile of v1, /device:TPU:16, one launch (start us, length us, event | category | flops | bytes accessed | tf_op | source)
XLA Modules:
  0.0 72.1 jit_solution(6224465889097617229)
XLA Ops:
  0.6 0.7 dynamic-slice_bitcast_fusion
  1.3 0.1 select_reduce_fusion.2
  1.5 0.1 select_reduce_fusion
  1.6 0.0 copy-start.1
  1.6 1.2 %copy-done.1 = bf16[1,512,1024]{2,1,0:T(8,128)(2,1)S(1)} copy-done((bf16[1,512,1024]{2,1,0:T(8,128)(2,1)S(1)}, bf16[1,512,1024]{2,1,0:T(8,128)(2,1)}, u32[]{:S(2)}) %copy-start.1) | copy-done | bytes 1048600
  2.8 0.0 copy-start.2
  2.8 1.2 %copy-done.2 = bf16[1,512,1024]{2,1,0:T(8,128)(2,1)S(1)} copy-done((bf16[1,512,1024]{2,1,0:T(8,128)(2,1)S(1)}, bf16[1,512,1024]{2,1,0:T(8,128)(2,1)}, u32[]{:S(2)}) %copy-start.2) | copy-done | bytes 1048600
  4.1 0.0 copy-start.3
  4.1 0.9 %copy-done.3 = bf16[1,512,256]{2,1,0:T(8,128)(2,1)S(1)} copy-done((bf16[1,512,256]{2,1,0:T(8,128)(2,1)S(1)}, bf16[1,512,256]{2,1,0:T(8,128)(2,1)}, u32[]{:S(2)}) %copy-start.3) | copy-done | bytes 262168
  5.0 0.0 copy-start.4
  5.0 0.9 %copy-done.4 = bf16[1,512,256]{2,1,0:T(8,128)(2,1)S(1)} copy-done((bf16[1,512,256]{2,1,0:T(8,128)(2,1)S(1)}, bf16[1,512,256]{2,1,0:T(8,128)(2,1)}, u32[]{:S(2)}) %copy-start.4) | copy-done | bytes 262168
  6.0 0.0 copy-start
  6.0 11.2 %attend.1 = (bf16[4,160,1024]{2,1,0:T(8,128)(2,1)S(1)}, bf16[4,160,256]{2,1,0:T(8,128)(2,1)S(1)}, bf16[4,160,256]{2,1,0:T(8,128)(2,1)S(1)}, bf16[512,256]{1,0:T(8,128)(2,1)S(1)}) custom-call(s32[4]{0:T(128)S(1)} %get-tuple-element.21.first_ref, s32[4]{0:T(128)S(1)} %get-tuple-element.20.len_ref, bf16[512,1024]{1,0:T(8,128)(2,1)S(1)} %bitcast.14, ...), custom_call_target="tpu_custom_call" | custom-call | tf_op jit(solution)/shard_map/attend/pallas_call | solution.py:223
  17.2 0.0 copy-done
  17.2 51.4 %exchange.1 = (bf16[4,160,1024]{2,1,0:T(8,128)(2,1)S(1)}, bf16[4,160,256]{2,1,0:T(8,128)(2,1)S(1)}, bf16[4,160,256]{2,1,0:T(8,128)(2,1)S(1)}, f32[256,1024]{1,0:T(8,128)S(1)}) custom-call(bf16[4,160,1024]{2,1,0:T(8,128)(2,1)S(1)} %get-tuple-element.12.dq_ref, bf16[4,160,256]{2,1,0:T(8,128)(2,1)S(1)} %get-tuple-element.13.dk_ref, ...), custom_call_target="tpu_custom_call" | custom-call | tf_op jit(solution)/shard_map/exchange/pallas_call | solution.py:239
  68.6 1.1 %copy.15 = bf16[1,640,1024]{2,1,0:T(8,128)(2,1)} copy(bf16[1,640,1024]{2,1,0:T(8,128)(2,1)S(1)} %bitcast.13) | data formatting | bytes 2621440
  69.7 0.7 %copy.16 = bf16[1,640,256]{2,1,0:T(8,128)(2,1)} copy(bf16[1,640,256]{2,1,0:T(8,128)(2,1)S(1)} %bitcast.17) | data formatting | bytes 655360
  70.4 0.7 %copy.17 = bf16[1,640,256]{2,1,0:T(8,128)(2,1)} copy(bf16[1,640,256]{2,1,0:T(8,128)(2,1)S(1)} %bitcast.16) | data formatting | bytes 655360
  71.1 1.0 %copy.18 = f32[256,1024]{1,0:T(8,128)} copy(f32[256,1024]{1,0:T(8,128)S(1)} %get-tuple-element.31) | data formatting | bytes 2097152
Async XLA Ops:
  1.6 1.2 %copy-start.1 = (bf16[1,512,1024]{2,1,0:T(8,128)(2,1)S(1)}, bf16[1,512,1024]{2,1,0:T(8,128)(2,1)}, u32[]{:S(2)}) copy-start(bf16[1,512,1024]{2,1,0:T(8,128)(2,1)} %param.7) | copy-start | bytes 3145732
  2.8 1.2 %copy-start.2 = (bf16[1,512,1024]{2,1,0:T(8,128)(2,1)S(1)}, bf16[1,512,1024]{2,1,0:T(8,128)(2,1)}, u32[]{:S(2)}) copy-start(bf16[1,512,1024]{2,1,0:T(8,128)(2,1)} %param.10) | copy-start | bytes 3145732
  4.1 0.9 %copy-start.3 = (bf16[1,512,256]{2,1,0:T(8,128)(2,1)S(1)}, bf16[1,512,256]{2,1,0:T(8,128)(2,1)}, u32[]{:S(2)}) copy-start(bf16[1,512,256]{2,1,0:T(8,128)(2,1)} %param.8) | copy-start | bytes 786436
  5.0 0.9 %copy-start.4 = (bf16[1,512,256]{2,1,0:T(8,128)(2,1)S(1)}, bf16[1,512,256]{2,1,0:T(8,128)(2,1)}, u32[]{:S(2)}) copy-start(bf16[1,512,256]{2,1,0:T(8,128)(2,1)} %param.9) | copy-start | bytes 786436
  6.0 11.2 %copy-start = (bf16[1,512,2048]{2,1,0:T(8,128)(2,1)S(1)}, bf16[1,512,2048]{2,1,0:T(8,128)(2,1)}, u32[]{:S(2)}) copy-start(bf16[1,512,2048]{2,1,0:T(8,128)(2,1)} %param.11) | copy-start | bytes 6291460

commit v2 on v1

--- a/solution.py
+++ b/solution.py
@@ -19,15 +19,54 @@
     return lax.dot_general(a, b, (((ca,), (cb,)), ((), ())), preferred_element_type=F32)
 
 
-def attend_kernel(first_ref, len_ref, q_ref, k_ref, v_ref, g_ref, dq_ref, dk_ref, dv_ref, tok_ref, acc):
-    n_blocks, cap = dq_ref.shape[0], dq_ref.shape[1]
-    seq_len = q_ref.shape[0]
+def fused_kernel(
+    n_dp, n_ctx, n_tp,
+    first_ref, len_ref, q_hbm, k_hbm, v_hbm, g_hbm, x_hbm,
+    q_out, k_out, v_out, w_out,
+    q_ref, k_ref, v_ref, g_ref, x_ref,
+    probs_s, qb_s, gb_s, kb_s, vb_s, dq_ref, dk_ref, dv_ref, acc, tok_ref,
+    xt, vals, a_send, a_recv, keep, b_send, b_recv, c_send, c_recv,
+    in_sem, own_sem, ctx_ssem, ctx_rsem, z_ssem, z_rsem, a_ssem, a_rsem, b_ssem, b_rsem, c_ssem, c_rsem,
+):
+    dp, ctx, tp = lax.axis_index("dp"), lax.axis_index("ctx"), lax.axis_index("tp")
+    n_far = n_ctx // 2
+    far, near = ctx // 2, ctx % 2
+    rows, width = keep.shape[3], keep.shape[4]
+
+    def ctx_at(p):
+        return (dp, lax.rem(ctx + p, n_ctx), tp)
+
+    def tp_at(p):
+        return (dp, ctx, lax.rem(tp + p, n_tp))
+
+    def dp_at(p):
+        return (lax.rem(dp + p, n_dp), ctx, tp)
+
+    loads = [
+        pltpu.make_async_copy(src, dst, in_sem.at[t])
+        for t, (src, dst) in enumerate(
+            ((k_hbm, k_ref), (q_hbm, q_ref), (v_hbm, v_ref), (g_hbm, g_ref), (x_hbm, x_ref)))
+    ]
+    for load in loads:
+        load.start()
+
+    barrier = pltpu.get_barrier_semaphore()
+    for p in range(1, n_ctx):
+        pl.semaphore_signal(barrier, inc=1, device_id=ctx_at(p), device_id_type=MESH)
+    for p in range(1, n_tp):
+        pl.semaphore_signal(barrier, inc=1, device_id=tp_at(p), device_id_type=MESH)
+    for p in range(1, n_dp):
+        pl.semaphore_signal(barrier, inc=1, device_id=dp_at(p), device_id_type=MESH)
+
+    cap, seq_len = dq_ref.shape[1], q_ref.shape[0]
     kv_local = k_ref.shape[1] // HD
     group = HEADS // KVH
     scale = HD ** (-0.5)
     acc[...] = jnp.zeros_like(acc)
-
-    def block(i, carry):
+    for load in loads[:4]:
+        load.wait()
+
+    def value_part(i, carry):
         first, length = first_ref[i], len_ref[i]
         row = lax.broadcasted_iota(jnp.int32, (cap, seq_len), 0)
         token = lax.broadcasted_iota(jnp.int32, (cap, seq_len), 1)
@@ -43,7 +82,6 @@
             kv = slice(n * HD, (n + 1) * HD)
             wide = slice(n * group * HD, (n + 1) * group * HD)
             kb = dot(pick, k_ref[:, kv], 1, 0).astype(BF16)
-            vb = dot(pick, v_ref[:, kv], 1, 0).astype(BF16)
             qw = dot(pick, q_ref[:, wide], 1, 0).astype(BF16)
             gw = dot(pick, g_ref[:, wide], 1, 0).astype(BF16)
             qb = jnp.concatenate([qw[:, h * HD:(h + 1) * HD] for h in range(group)], axis=0)
@@ -51,52 +89,34 @@
             scores = jnp.where(allowed, dot(qb, kb, 1, 1) * scale, -jnp.inf)
             raised = jnp.exp(scores - jnp.max(scores, axis=1, keepdims=True))
             probs = raised / jnp.sum(raised, axis=1, keepdims=True)
-            low = probs.astype(BF16)
-            prob_grad = dot(gb, vb, 1, 1)
-            delta = jnp.sum(low.astype(F32) * prob_grad, axis=1, keepdims=True)
+            dv = dot(probs.astype(BF16), gb, 0, 0).astype(BF16)
+            dv_ref[i, :, kv] = dv
+            acc[:, kv] += dot(place, dv, 1, 0)
+            vb_s[i, n] = dot(pick, v_ref[:, kv], 1, 0).astype(BF16)
+            probs_s[i, n] = probs
+            qb_s[i, n] = qb
+            gb_s[i, n] = gb
+            kb_s[i, n] = kb
+        return carry
+
+    lax.fori_loop(0, n_ctx, value_part, 0)
+    tok_ref[...] = acc[...].astype(BF16)
+
+    def query_key_part(i):
+        for n in range(kv_local):
+            kv = slice(n * HD, (n + 1) * HD)
+            probs = probs_s[i, n]
+            kb = kb_s[i, n]
+            prob_grad = dot(gb_s[i, n], vb_s[i, n], 1, 1)
+            low = probs.astype(BF16).astype(F32)
+            delta = jnp.sum(low * prob_grad, axis=1, keepdims=True)
             dscore = (probs * (prob_grad - delta)).astype(BF16)
             dq = (dot(dscore, kb, 1, 0) * scale).astype(BF16)
             for h in range(group):
                 at = (n * group + h) * HD
                 dq_ref[i, :, at:at + HD] = dq[h * cap:(h + 1) * cap]
-            dk_ref[i, :, kv] = (dot(dscore, qb, 0, 0) * scale).astype(BF16)
-            dv = dot(low, gb, 0, 0).astype(BF16)
-            dv_ref[i, :, kv] = dv
-            acc[:, kv] += dot(place, dv, 1, 0)
-        return carry
-
-    lax.fori_loop(0, n_blocks, block, 0)
-    tok_ref[...] = acc[...].astype(BF16)
-
-
-def exchange_kernel(
-    n_dp, n_ctx, n_tp,
-    dq_ref, dk_ref, dv_ref, tok_ref, x_ref,
-    q_out, k_out, v_out, w_out,
-    xt, vals, a_send, a_recv, keep, b_send, b_recv, c_send, c_recv,
-    own_sem, ctx_ssem, ctx_rsem, z_ssem, z_rsem, a_ssem, a_rsem, b_ssem, b_rsem, c_ssem, c_rsem,
-):
-    dp, ctx, tp = lax.axis_index("dp"), lax.axis_index("ctx"), lax.axis_index("tp")
-    n_far = n_ctx // 2
-    far, near = ctx // 2, ctx % 2
-    rows, width = keep.shape[3], keep.shape[4]
-
-    def ctx_at(p):
-        return (dp, lax.rem(ctx + p, n_ctx), tp)
-
-    def tp_at(p):
-        return (dp, ctx, lax.rem(tp + p, n_tp))
-
-    def dp_at(p):
-        return (lax.rem(dp + p, n_dp), ctx, tp)
-
-    barrier = pltpu.get_barrier_semaphore()
-    for p in range(1, n_ctx):
-        pl.semaphore_signal(barrier, inc=1, device_id=ctx_at(p), device_id_type=MESH)
-    for p in range(1, n_tp):
-        pl.semaphore_signal(barrier, inc=1, device_id=tp_at(p), device_id_type=MESH)
-    for p in range(1, n_dp):
-        pl.semaphore_signal(barrier, inc=1, device_id=dp_at(p), device_id_type=MESH)
+            dk_ref[i, :, kv] = (dot(dscore, qb_s[i, n], 0, 0) * scale).astype(BF16)
+
     pl.semaphore_wait(barrier, n_ctx + n_tp + n_dp - 3)
 
     def remote(src, dst, ssem, rsem, device):
@@ -111,19 +131,23 @@
     for p in order[1:]:
         gathers[p] = remote(tok_ref, vals.at[p], z_ssem.at[p], z_rsem.at[p], tp_at(p))
         gathers[p].start()
-    moves = []
-    for p in range(1, n_ctx):
+    def move(t, p):
+        src, dst = ((dq_ref, q_out), (dk_ref, k_out), (dv_ref, v_out))[t]
         dest = lax.rem(ctx + p, n_ctx)
-        for t, (src, dst) in enumerate(((dq_ref, q_out), (dk_ref, k_out), (dv_ref, v_out))):
-            move = remote(src.at[dest], dst.at[ctx], ctx_ssem.at[t, p], ctx_rsem.at[t, p], ctx_at(p))
-            move.start()
-            moves.append(move)
-    owns = []
-    for t, (src, dst) in enumerate(((dq_ref, q_out), (dk_ref, k_out), (dv_ref, v_out))):
-        own = pltpu.make_async_copy(src.at[ctx], dst.at[ctx], own_sem.at[t])
-        own.start()
-        owns.append(own)
-
+        return remote(src.at[dest], dst.at[ctx], ctx_ssem.at[t, p], ctx_rsem.at[t, p], ctx_at(p))
+
+    def own(t):
+        src, dst = ((dq_ref, q_out), (dk_ref, k_out), (dv_ref, v_out))[t]
+        return pltpu.make_async_copy(src.at[ctx], dst.at[ctx], own_sem.at[t])
+
+    def send_block(p, carry):
+        query_key_part(lax.rem(ctx + p, n_ctx))
+        for t in range(3):
+            move(t, p).start()
+        return carry
+
+    lax.fori_loop(1, n_ctx, send_block, 0)
+    loads[4].wait()
     for b in range(n_dp * n_ctx):
         xt[b] = x_ref[:, b * rows:(b + 1) * rows].T
 
@@ -186,11 +210,15 @@
         for lag, stage in ((3, stage_last), (2, stage_far), (1, stage_dp), (0, stage_near)):
             if 0 <= u - lag < n_tp:
                 stage(u - lag)
-
-    for own in owns:
-        own.wait()
-    for move in moves:
-        move.wait()
+        if u == 0:
+            query_key_part(ctx)
+            for t in range(3):
+                own(t).start()
+
+    for t in range(3):
+        own(t).wait()
+        for p in range(1, n_ctx):
+            move(t, p).wait()
     for p in order[1:]:
         gathers[p].wait_send()
     for u in range(n_tp):
@@ -217,36 +245,38 @@
     send_len = jnp.sum(jnp.where(chosen, lengths[None, :], 0), axis=1)
     send_first = jnp.sum(jnp.where(chosen, starts[None, :], 0), axis=1)
 
+    kv_local = kv_width // HD
+    stacked = HEADS // KVH * padded
     vmem = pl.BlockSpec(memory_space=pltpu.VMEM)
     smem = pl.BlockSpec(memory_space=pltpu.SMEM)
     anywhere = pl.BlockSpec(memory_space=pl.ANY)
-    dq, dk, dv, tok = pl.pallas_call(
-        attend_kernel,
+    dma = pltpu.SemaphoreType.DMA
+    q_out, k_out, v_out, w_out = pl.pallas_call(
+        functools.partial(fused_kernel, n_dp, n_ctx, n_tp),
         out_shape=(
             jax.ShapeDtypeStruct((n_ctx, padded, q_width), BF16),
             jax.ShapeDtypeStruct((n_ctx, padded, kv_width), BF16),
             jax.ShapeDtypeStruct((n_ctx, padded, kv_width), BF16),
-            jax.ShapeDtypeStruct((seq_len, kv_width), BF16),
-        ),
-        in_specs=[smem, smem, vmem, vmem, vmem, vmem],
-        out_specs=(vmem, vmem, vmem, vmem),
-        scratch_shapes=[pltpu.VMEM((seq_len, kv_width), F32)],
-        compiler_params=pltpu.CompilerParams(vmem_limit_bytes=32 << 20),
-        name="attend",
-    )(send_first, send_len, queries[0], key_rows[0], value_rows[0], out_grad[0])
-
-    dma = pltpu.SemaphoreType.DMA
-    q_out, k_out, v_out, w_out = pl.pallas_call(
-        functools.partial(exchange_kernel, n_dp, n_ctx, n_tp),
-        out_shape=(
-            jax.ShapeDtypeStruct(dq.shape, BF16),
-            jax.ShapeDtypeStruct(dk.shape, BF16),
-            jax.ShapeDtypeStruct(dv.shape, BF16),
             jax.ShapeDtypeStruct((rows, n_tp * kv_width), F32),
         ),
-        in_specs=[anywhere, anywhere, anywhere, vmem, vmem],
+        in_specs=[smem, smem] + [anywhere] * 5,
         out_specs=(anywhere, anywhere, anywhere, vmem),
         scratch_shapes=[
+            pltpu.VMEM((seq_len, q_width), BF16),
+            pltpu.VMEM((seq_len, kv_width), BF16),
+            pltpu.VMEM((seq_len, kv_width), BF16),
+            pltpu.VMEM((seq_len, q_width), BF16),
+            pltpu.VMEM((seq_len, features), BF16),
+            pltpu.VMEM((n_ctx, kv_local, stacked, padded), F32),
+            pltpu.VMEM((n_ctx, kv_local, stacked, HD), BF16),
+            pltpu.VMEM((n_ctx, kv_local, stacked, HD), BF16),
+            pltpu.VMEM((n_ctx, kv_local, padded, HD), BF16),
+            pltpu.VMEM((n_ctx, kv_local, padded, HD), BF16),
+            pltpu.VMEM((n_ctx, padded, q_width), BF16),
+            pltpu.VMEM((n_ctx, padded, kv_width), BF16),
+            pltpu.VMEM((n_ctx, padded, kv_width), BF16),
+            pltpu.VMEM((seq_len, kv_width), F32),
+            pltpu.VMEM((seq_len, kv_width), BF16),
             pltpu.VMEM((n_dp * n_ctx, rows, seq_len), BF16),
             pltpu.VMEM((n_tp, seq_len, kv_width), BF16),
             pltpu.VMEM((n_tp, n_dp, n_far, rows, kv_width), BF16),
@@ -256,6 +286,7 @@
             pltpu.VMEM((n_tp, n_dp, n_far, rows, kv_width), BF16),
             pltpu.VMEM((n_tp, n_far, rows, kv_width), BF16),
             pltpu.VMEM((n_tp, n_far, rows, kv_width), BF16),
+            dma((5,)),
             dma((3,)),
             dma((3, n_ctx)), dma((3, n_ctx)),
             dma((n_tp,)), dma((n_tp,)),
@@ -264,9 +295,9 @@
             dma((n_tp, n_far)), dma((n_tp, n_far)),
         ],
         compiler_params=pltpu.CompilerParams(
-            collective_id=0, has_side_effects=True, vmem_limit_bytes=40 << 20),
-        name="exchange",
-    )(dq, dk, dv, tok, inputs[0])
+            collective_id=0, has_side_effects=True, vmem_limit_bytes=56 << 20),
+        name="fused",
+    )(send_first, send_len, queries[0], key_rows[0], value_rows[0], out_grad[0], inputs[0])
 
     def joined(block):
         return block[:, :capacity].reshape(1, n_ctx * capacity, block.shape[2])

time: 72.4 us -> 68.5 us (0.946)
  local copies, waits for them, and re-layouts: 8.54 us -> 5.67 us
  Pallas kernels: 62.6 us -> 61.2 us
    unnamed x14 -> x10, local copies, waits for them, and re-layouts: 7.83 us -> 4.96 us
    pallas_call x2 -> x1, Pallas kernels: 62.6 us -> 61.2 us  [shards(): pl.pallas_call(functools.partial(fused_kernel, n_dp, n_ctx, n_tp), out_sh...]
where the time goes in v2:
time: 68.5 us; the launch traced here: 68.3 us
  Pallas kernels  61.2 us (89%)
  local copies, waits for them, and re-layouts  5.67 us (8%)
  other arithmetic  0.78 us (1%)
    pallas_call x1, Pallas kernels, shards(): pl.pallas_call(functools.partial(fused_kernel, n_dp, n_ctx, n_tp), out_sh...  61.2 us
    unnamed x10, local copies, waits for them, and re-layouts  4.96 us

profile of v2, /device:TPU:16, one launch (start us, length us, event | category | flops | bytes accessed | tf_op | source)
XLA Modules:
  0.0 68.3 jit_solution(10079687933461829101)
XLA Ops:
  0.6 0.7 %dynamic-slice_bitcast_fusion = (s32[4]{0:T(128)S(1)}, s32[4]{0:T(128)S(1)}) fusion(s32[4,4]{1,0:T(4,128)} %param.12, s32[]{:T(128)S(6)} %select_n.15, s32[4,4]{1,0:T(4,128)} %param.13), kind=kLoop, calls=%fused_computation.5 | loop fusion | bytes 68 | tf_op jit(solution)/shard_map/jit(_where)/broadcast_in_dim | solution.py:243
  1.3 0.1 select_reduce_fusion.2
  1.5 0.7 select_reduce_fusion
  2.1 61.2 %fused.1 = (bf16[4,160,1024]{2,1,0:T(8,128)(2,1)}, bf16[4,160,256]{2,1,0:T(8,128)(2,1)}, bf16[4,160,256]{2,1,0:T(8,128)(2,1)}, f32[256,1024]{1,0:T(8,128)}) custom-call(s32[4]{0:T(128)} %get-tuple-element.13.first_ref, s32[4]{0:T(128)} %get-tuple-element.12.len_ref, bf16[512,1024]{1,0:T(8,128)(2,1)} %bitcast.14, bf16[512,256]{1,0:T(8,128)(2,1)} %bitcast.18, ...), custom_call_target="tpu_custom_call" | custom-call | tf_op jit(solution)/shard_map/fused/pallas_call | solution.py:254
  63.3 0.0 copy-start.2
  63.4 0.0 copy-start.1
  63.4 2.5 %copy.15 = bf16[1,640,1024]{2,1,0:T(8,128)(2,1)} copy(bf16[1,640,1024]{2,1,0:T(8,128)(2,1)} %bitcast.13) | data formatting | bytes 2621440
  65.9 0.0 copy-done.2
  65.9 0.0 copy-start
  65.9 0.7 %copy.16 = bf16[1,640,256]{2,1,0:T(8,128)(2,1)} copy(bf16[1,640,256]{2,1,0:T(8,128)(2,1)S(1)} %bitcast.17) | data formatting | bytes 655360
  66.6 0.0 copy-done.1
  66.6 0.7 %copy.17 = bf16[1,640,256]{2,1,0:T(8,128)(2,1)} copy(bf16[1,640,256]{2,1,0:T(8,128)(2,1)S(1)} %bitcast.16) | data formatting | bytes 655360
  67.4 0.0 copy-done
  67.4 1.0 %copy.18 = f32[256,1024]{1,0:T(8,128)} copy(f32[256,1024]{1,0:T(8,128)S(1)} %copy-done) | data formatting | bytes 2097152
Async XLA Ops:
  63.3 2.6 %copy-start.2 = (bf16[4,160,256]{2,1,0:T(8,128)(2,1)S(1)}, bf16[4,160,256]{2,1,0:T(8,128)(2,1)}, u32[]{:S(2)}) copy-start(bf16[4,160,256]{2,1,0:T(8,128)(2,1)} %get-tuple-element.9) | copy-start | bytes 983044
  63.4 3.3 %copy-start.1 = (bf16[4,160,256]{2,1,0:T(8,128)(2,1)S(1)}, bf16[4,160,256]{2,1,0:T(8,128)(2,1)}, u32[]{:S(2)}) copy-start(bf16[4,160,256]{2,1,0:T(8,128)(2,1)} %get-tuple-element.10) | copy-start | bytes 983044
  65.9 1.5 %copy-start = (f32[256,1024]{1,0:T(8,128)S(1)}, f32[256,1024]{1,0:T(8,128)}, u32[]{:S(2)}) copy-start(f32[256,1024]{1,0:T(8,128)} %get-tuple-element.23) | copy-start | bytes 3145732
